TPU v7x, 32 devices: a whole 2x2x4 slice. The times are simulated.
32 devices in a mesh: dp: 8 (over z, x), tensor: 4 (over y, core).
Axes of the slice: x: 2, y: 2, z: 4, core: 2. Of those that a mesh axis runs over, the one named last changes fastest.
Arguments:
- context: bfloat16 [4096, 4096], P('dp', 'tensor'), may hold values from -134 to 134, as said below
- latents: bfloat16 [4096, 4096], P('dp', 'tensor'), may hold values from -12 to 12, as said below
- gain_ctx: float32 [4096], replicated, may hold values from 0.1 to 1.9
- gain_lat: float32 [4096], replicated, may hold values from 0.1 to 1.9
- w_query: bfloat16 [4096, 1536], P(None, 'tensor'), may hold values from -0.09375 to 0.09375
- key_matrix: bfloat16 [4096, 384], P(None, 'tensor'), may hold values from -0.09375 to 0.09375
- value_matrix: bfloat16 [4096, 384], P(None, 'tensor'), may hold values from -0.09375 to 0.09375
- w_out: bfloat16 [4096, 1536], P(None, 'tensor'), may hold values from -1 to 1
- lengths: int32 [8, 8], P('dp'), may hold values from 1 to 128, 512 in all within a row
- patch_flags: int32 [4096], P('dp'), may hold values 0 or 1
- cotangent: bfloat16 [4096, 4096], P('dp', 'tensor'), may hold values from -6 to 6
Outputs:
- latents_out: bfloat16 [4096, 4096], P('dp', 'tensor')
- grad_context: bfloat16 [4096, 4096], P('dp', 'tensor')
- grad_latents: bfloat16 [4096, 4096], P('dp', 'tensor')
- grad_w_query: float32 [4096, 1536], P('dp', 'tensor')
- grad_w_key: float32 [4096, 384], P('dp', 'tensor')
- grad_w_value: float32 [4096, 384], P('dp', 'tensor')
- grad_w_out: float32 [4096, 1536], P('dp', 'tensor')
- grad_gain_ctx: float32 [4, 1024], P('tensor', 'dp')
- grad_gain_lat: float32 [4, 1024], P('tensor', 'dp')
Inputs may be any that keep to these rules, and one draw needn't show every extreme that they name: `lengths`: row b lists, in order, the patch counts of the 8 images whose patches fill rows b * 512 to (b + 1) * 512 - 1 of context; every row sums to 512. `context`: real values. `latents`: real values.
All inputs are finite; a program needn't handle non-finite values. No bound on the sum of `patch_flags` on one device may be relied on, other than what follows from the above.
Results may differ from a plain program's by a relative error of at most 0.013.
Values may be sent and summed in bfloat16 or wider, within the bound.
A program may use at most 192 MiB of HBM per device.

v0:
```python
import functools

import jax
import jax.numpy as jnp
from jax import lax
from jax.experimental import pallas as pl
from jax.experimental.pallas import tpu as pltpu
from jax.sharding import PartitionSpec as P

HEAD_DIM = 96
LAT = 64


epsilon = 1e-06
masked_value = -1e30
contract_rows = (((0,), (0,)), ((), ()))
contract_cols = (((1,), (1,)), ((), ()))


def row_scales(rows_in):
    values_f = rows_in.astype(jnp.float32)
    return (values_f, lax.rsqrt(jnp.mean(values_f * values_f, axis=1) + epsilon))


def norm_back(grad_norm, local_vals, row_scale, gain_local, row_inner_all, model_width):
    weighted = grad_norm * gain_local
    grad_input = (
        row_scale[:, None] * weighted
        - local_vals * (row_scale**3 * row_inner_all / model_width)[:, None]
    )
    grad_gain = jnp.sum(grad_norm * local_vals * row_scale[:, None], axis=0)
    return (grad_input, grad_gain)


def plain_local(
    context,
    latents,
    gain_ctx,
    gain_lat,
    w_query,
    key_matrix,
    value_matrix,
    w_out,
    lengths,
    patch_flags,
    cotangent,
):
    patch_rows = context.shape[0]
    latent_rows = latents.shape[0]
    local_width = context.shape[1]
    model_width = gain_ctx.shape[0]
    head_size = HEAD_DIM
    kv_local = key_matrix.shape[1] // head_size
    query_local = w_query.shape[1] // head_size
    repeat = query_local // kv_local
    all_count = patch_rows + latent_rows
    score_scale = head_size ** (-0.5)
    column = lax.axis_index("tensor") * local_width
    whole_ctx, whole_lat = (
        lax.all_gather(context, "tensor", axis=1, tiled=True),
        lax.all_gather(latents, "tensor", axis=1, tiled=True),
    )
    ctx_values, ctx_scale = row_scales(whole_ctx)
    lat_values, lat_scale = row_scales(whole_lat)
    ctx_norm = (ctx_values * ctx_scale[:, None] * gain_ctx).astype(jnp.bfloat16)
    lat_norm = (lat_values * lat_scale[:, None] * gain_lat).astype(jnp.bfloat16)
    queries = jnp.dot(lat_norm, w_query, preferred_element_type=jnp.float32).astype(jnp.bfloat16)
    all_rows = jnp.concatenate([ctx_norm, lat_norm], axis=0)
    w_pair = jnp.concatenate([key_matrix, value_matrix], axis=1)
    pair_rows = jnp.dot(all_rows, w_pair, preferred_element_type=jnp.float32).astype(jnp.bfloat16)
    key_head_split = (
        pair_rows[:, : kv_local * head_size]
        .reshape(all_count, kv_local, head_size)
        .transpose(1, 0, 2)
    )
    value_head_split = (
        pair_rows[:, kv_local * head_size :]
        .reshape(all_count, kv_local, head_size)
        .transpose(1, 0, 2)
    )
    query_heads = queries.reshape(latent_rows, query_local, head_size).transpose(1, 0, 2)
    image_ends = jnp.cumsum(lengths[0])
    patch_image = jnp.sum(
        (jnp.arange(patch_rows)[:, None] >= image_ends[None, :]).astype(jnp.int32), axis=1
    )
    latent_image = jnp.arange(latent_rows) // LAT
    allowed = jnp.concatenate(
        [
            (latent_image[:, None] == patch_image[None, :]) & (patch_flags[None, :] == 1),
            latent_image[:, None] == latent_image[None, :],
        ],
        axis=1,
    )
    head_index = jnp.arange(query_local)

    def head_scores(query_head, head_number):
        key_head = key_head_split[head_number // repeat]
        value_head = value_head_split[head_number // repeat]
        raw_scores = (
            lax.dot_general(query_head, key_head, contract_cols, preferred_element_type=jnp.float32)
            * score_scale
        )
        return (jnp.where(allowed, raw_scores, masked_value), key_head, value_head)

    def head_forward(member):
        query_head, head_number = member
        scores, key_head, value_head = head_scores(query_head, head_number)
        row_top = jnp.max(scores, axis=1, keepdims=True)
        exp_scores = jnp.exp(scores - row_top)
        row_total = jnp.sum(exp_scores, axis=1, keepdims=True)
        attention = (exp_scores / row_total).astype(jnp.bfloat16)
        blended = jnp.dot(attention, value_head, preferred_element_type=jnp.float32).astype(
            jnp.bfloat16
        )
        return (blended, row_top[:, 0] + jnp.log(row_total[:, 0]))

    heads_out, log_totals = lax.map(head_forward, (query_heads, head_index))
    attended = heads_out.transpose(1, 0, 2).reshape(latent_rows, query_local * head_size)
    partial_out = lax.dot_general(
        attended, w_out, contract_cols, preferred_element_type=jnp.float32
    )
    branch = lax.psum_scatter(
        partial_out.astype(jnp.bfloat16), "tensor", scatter_dimension=1, tiled=True
    ).astype(jnp.float32)
    latents_out = (latents.astype(jnp.float32) + branch).astype(jnp.bfloat16)
    full_grad = lax.all_gather(cotangent, "tensor", axis=1, tiled=True)
    grad_attended = jnp.dot(full_grad, w_out, preferred_element_type=jnp.float32).astype(
        jnp.bfloat16
    )
    grad_w_out = lax.dot_general(
        full_grad, attended, contract_rows, preferred_element_type=jnp.float32
    )
    grad_heads = grad_attended.reshape(latent_rows, query_local, head_size).transpose(1, 0, 2)

    def head_backward(member):
        query_head, grad_blended, log_total, head_number = member
        scores, key_head, value_head = head_scores(query_head, head_number)
        attention = jnp.exp(scores - log_total[:, None])
        grad_probs = lax.dot_general(
            grad_blended, value_head, contract_cols, preferred_element_type=jnp.float32
        )
        row_inner = jnp.sum(attention * grad_probs, axis=1, keepdims=True)
        grad_scores = (attention * (grad_probs - row_inner)).astype(jnp.bfloat16)
        grad_query = (
            jnp.dot(grad_scores, key_head, preferred_element_type=jnp.float32) * score_scale
        ).astype(jnp.bfloat16)
        grad_key = (
            lax.dot_general(
                grad_scores, query_head, contract_rows, preferred_element_type=jnp.float32
            )
            * score_scale
        )
        grad_value = lax.dot_general(
            attention.astype(jnp.bfloat16),
            grad_blended,
            contract_rows,
            preferred_element_type=jnp.float32,
        )
        return (grad_query, grad_key, grad_value)

    grad_query_heads, grad_key_heads, grad_value_heads = lax.map(
        head_backward, (query_heads, grad_heads, log_totals, head_index)
    )
    grad_keys = grad_key_heads.reshape(kv_local, repeat, all_count, head_size).sum(axis=1)
    grad_values = grad_value_heads.reshape(kv_local, repeat, all_count, head_size).sum(axis=1)
    grad_pair = jnp.concatenate(
        [
            grad_keys.transpose(1, 0, 2).reshape(all_count, kv_local * head_size),
            grad_values.transpose(1, 0, 2).reshape(all_count, kv_local * head_size),
        ],
        axis=1,
    ).astype(jnp.bfloat16)
    grad_q_rows = grad_query_heads.transpose(1, 0, 2).reshape(latent_rows, query_local * head_size)
    grad_w_query = lax.dot_general(
        lat_norm, grad_q_rows, contract_rows, preferred_element_type=jnp.float32
    )
    grad_w_pair = lax.dot_general(
        all_rows, grad_pair, contract_rows, preferred_element_type=jnp.float32
    )
    grad_rows = lax.dot_general(
        grad_pair, w_pair, contract_cols, preferred_element_type=jnp.float32
    )
    lat_terms = grad_rows[patch_rows:] + lax.dot_general(
        grad_q_rows, w_query, contract_cols, preferred_element_type=jnp.float32
    )
    grad_ctx_norm, grad_lat_norm = (
        lax.psum_scatter(
            grad_rows[:patch_rows].astype(jnp.bfloat16), "tensor", scatter_dimension=1, tiled=True
        ).astype(jnp.float32),
        lax.psum_scatter(
            lat_terms.astype(jnp.bfloat16), "tensor", scatter_dimension=1, tiled=True
        ).astype(jnp.float32),
    )
    ctx_local = context.astype(jnp.float32)
    lat_local = latents.astype(jnp.float32)
    gain_ctx_local = lax.dynamic_slice_in_dim(gain_ctx, column, local_width, 0)
    gain_lat_local = lax.dynamic_slice_in_dim(gain_lat, column, local_width, 0)
    ctx_inner = jnp.sum(grad_ctx_norm * gain_ctx_local * ctx_local, axis=1)
    lat_inner = jnp.sum(grad_lat_norm * gain_lat_local * lat_local, axis=1)
    ctx_inner_all, lat_inner_all = lax.psum((ctx_inner, lat_inner), "tensor")
    grad_ctx_in, grad_gain_c = norm_back(
        grad_ctx_norm, ctx_local, ctx_scale, gain_ctx_local, ctx_inner_all, model_width
    )
    grad_lat_in, grad_gain_l = norm_back(
        grad_lat_norm, lat_local, lat_scale, gain_lat_local, lat_inner_all, model_width
    )
    grad_context = grad_ctx_in.astype(jnp.bfloat16)
    grad_latents = (cotangent.astype(jnp.float32) + grad_lat_in).astype(jnp.bfloat16)
    grad_w_key = grad_w_pair[:, : kv_local * head_size]
    grad_w_value = grad_w_pair[:, kv_local * head_size :]
    sum_query, sum_key, sum_value, sum_out, sum_gain_c, sum_gain_l = (
        lax.psum_scatter(grad_w_query, "dp", scatter_dimension=0, tiled=True),
        lax.psum_scatter(grad_w_key, "dp", scatter_dimension=0, tiled=True),
        lax.psum_scatter(grad_w_value, "dp", scatter_dimension=0, tiled=True),
        lax.psum_scatter(grad_w_out, "dp", scatter_dimension=0, tiled=True),
        lax.psum_scatter(grad_gain_c, "dp", scatter_dimension=0, tiled=True),
        lax.psum_scatter(grad_gain_l, "dp", scatter_dimension=0, tiled=True),
    )
    return (
        latents_out,
        grad_context,
        grad_latents,
        sum_query,
        sum_key,
        sum_value,
        sum_out,
        sum_gain_c.reshape(1, -1),
        sum_gain_l.reshape(1, -1),
    )


MESH = pl.DeviceIdType.MESH
f32 = jnp.float32
bf16 = jnp.bfloat16
ROWS = 128
LOG2_E = 1.4426950408889634


def nn(a, b):
    return jnp.dot(a, b, preferred_element_type=f32)


def nt(a, b):
    return lax.dot_general(a, b, contract_cols, preferred_element_type=f32)


def flip(a):
    return a.astype(f32).T.astype(bf16)


def block_kernel(
    n_dp,
    context,
    latents,
    cotangent,
    gain_ctx_in,
    gain_lat_in,
    w_query,
    key_across,
    value_across,
    w_out,
    lengths_in,
    flags_in,
    out_latents,
    out_context,
    out_grad_lat,
    out_query,
    out_key,
    out_value,
    out_out,
    out_gain_c,
    out_gain_l,
    gain_ctx,
    gain_lat,
    lengths,
    flags,
    gain_out,
    lat_all,
    cot_all,
    ctx_own,
    raw_lat,
    raw_ctx,
    wq,
    wkv,
    w_own,
    wo,
    acc_q,
    kv_acc,
    att_t,
    sgq_t,
    q_rows,
    q_cols,
    ga_rows,
    ga_cols,
    k_rows,
    v_rows,
    far_s,
    near_s,
    far_g,
    near_g,
    att,
    sgq,
    kv_t,
    kv_send,
    kv_core,
    kv_y,
    probs_c,
    probs_l,
    gkv,
    sgkv_all,
    sgc,
    sgl,
    sums,
    inners,
    scale_row,
    coef_row,
    gain_part,
    gain_sum,
    gain_recv,
    gain_all,
    core_send,
    core_recv,
    y_recv,
    lat_x,
    cot_x,
    att_xt,
    sgq_xt,
    z_send_o,
    z_send_q,
    z_recv_o,
    z_recv_q,
    x_send_kv,
    x_recv_kv,
    z_recv_kv,
    own_send,
    own_recv,
    dp_acc,
    send_sem,
    recv_sem,
    local_sem,
):
    rows, width = raw_lat.shape
    n_rows = rows // ROWS
    n_hi = n_dp // 2
    feat = 4 * width // n_dp
    head = HEAD_DIM
    heads = acc_q.shape[1] // head
    model_width = 4 * width
    score_scale = head ** (-0.5)

    dp = lax.axis_index("dp")
    f = lax.axis_index("tensor")
    z, x = dp // 2, lax.rem(dp, 2)
    y, c = f // 2, lax.rem(f, 2)
    f_c = y * 2 + (1 - c)
    f_y = (1 - y) * 2 + c
    f_yc = (1 - y) * 2 + (1 - c)
    core_dev, y_dev, yc_dev = (dp, f_c), (dp, f_y), (dp, f_yc)
    x_dev = (z * 2 + 1 - x, f)
    z_1 = z + 1 - 2 * lax.rem(z, 2)
    z_2 = z + 2 - 4 * (z // 2)
    z1_dev, z2_dev = (z_1 * 2 + x, f), (z_2 * 2 + x, f)
    x_mine = pl.ds(pl.multiple_of(x * feat, 128), feat)
    x_other = pl.ds(pl.multiple_of((1 - x) * feat, 128), feat)

    urgent = lax.rem(c + z, 2) == 1
    patient = jnp.logical_not(urgent)

    count = [0]

    def take(n):
        count[0] += n
        return count[0] - n

    def remote(src, dst, sem, dev, sem_to=None):
        return pltpu.make_async_remote_copy(
            src_ref=src,
            dst_ref=dst,
            send_sem=send_sem.at[sem],
            recv_sem=recv_sem.at[sem if sem_to is None else sem_to],
            device_id=dev,
            device_id_type=MESH,
        )

    def local_copy(src, dst, i):
        return pltpu.make_async_copy(src, dst, local_sem.at[i])

    def part_rows(k):
        if isinstance(k, int):
            return pl.ds(k * ROWS, ROWS)
        return pl.ds(pl.multiple_of(k * ROWS, ROWS), ROWS)

    n_cols = 4
    piece = width // n_cols

    def part_cols(k):
        if isinstance(k, int):
            return pl.ds(k * piece, piece)
        return pl.ds(pl.multiple_of(k * piece, 128), piece)

    def cols_at(fb, k):
        return pl.ds(pl.multiple_of(fb * width + k * piece, 128), piece)

    def block_cols(fb):
        if isinstance(fb, int):
            return pl.ds(fb * width, width)
        return pl.ds(pl.multiple_of(fb * width, width), width)

    loads = [
        local_copy(latents, raw_lat, 0),
        local_copy(key_across, wkv.at[pl.ds(0, head)], 4),
        local_copy(value_across, wkv.at[pl.ds(head, head)], 14),
        local_copy(context, raw_ctx, 1),
        local_copy(cotangent, cot_all.at[f], 13),
        local_copy(w_query, wq, 3),
        local_copy(w_out, wo, 5),
    ]
    small = [
        local_copy(gain_lat_in, gain_lat, 2),
        local_copy(gain_ctx_in, gain_ctx, 6),
        local_copy(lengths_in, lengths, 7),
        local_copy(flags_in, flags, 8),
    ]
    for load in small[:1] + loads + small[1:]:
        load.start()

    barrier = pltpu.get_barrier_semaphore()

    def greet(dev):
        pl.semaphore_signal(barrier, inc=1, device_id=dev, device_id_type=MESH)

    others = [i for i in range(1, n_hi)]

    def far_dev(i):
        return (lax.rem(z + i, n_hi) * 2 + x, f)

    def far_x_dev(i):
        return (lax.rem(z + i, n_hi) * 2 + 1 - x, f)

    always = [core_dev, y_dev, yc_dev, x_dev] + [far_dev(i) for i in others]
    always += [far_x_dev(i) for i in others]
    for dev in always:
        greet(dev)
    pl.when(z != f)(lambda: greet((z_2 * 2 + x, z)))

    def weigh(raw, gain, buf):
        gain_row = gain[:, block_cols(f)]
        for k in range(n_rows):
            values = raw[part_rows(k), :].astype(f32)
            buf[part_rows(k), :] = (values * gain_row).astype(bf16)

    small[0].wait()
    loads[0].wait()
    weigh(raw_lat, gain_lat, lat_all.at[f])
    middle = z_2 == f
    pl.semaphore_wait(barrier, len(always) + 3 * middle.astype(jnp.int32))

    sem_lat, sem_cot = (take(2 * n_rows + 1) for _ in range(2))

    def gather_y(buf, base, k):
        return remote(buf.at[f, part_rows(k)], buf.at[f, part_rows(k)], base + k, y_dev)

    def gather_core(buf, base):
        return remote(buf.at[f], buf.at[f], base + n_rows, core_dev)

    def gather_on(buf, base, k):
        return remote(
            buf.at[f_y, part_rows(k)], buf.at[f_y, part_rows(k)], base + n_rows + 1 + k, core_dev
        )

    def pass_on(buf, base, held=None, base_x=None):
        def step(k, carry):
            gather_y(buf, base, k).wait_recv()
            gather_on(buf, base, k).start()
            if held is not None:
                rows_x(buf, held, base_x, k).start()
            return carry

        lax.fori_loop(0, n_rows, step, 0)

    def wait_on(buf, base):
        for k in range(n_rows):
            gather_on(buf, base, k).wait_recv()

    def gather_done(buf, base):
        for k in range(n_rows):
            gather_y(buf, base, k).wait_send()
            gather_on(buf, base, k).wait_send()
        gather_core(buf, base).wait_send()

    def square_sums(raw, index):
        for k in range(n_rows):
            values = raw[part_rows(k), :].astype(f32)
            total = jnp.sum(values * values, axis=1, keepdims=True)
            across = jnp.broadcast_to(total, (ROWS, 128)).T
            sums[f, pl.ds(index, 1), part_rows(k)] = across[0:1, :]

    sem_lat_x, sem_cot_x = take(2 * n_rows + 2), take(2 * n_rows + 2)
    sem_att_x, sem_sgq_x = take(n_rows), take(n_rows)

    def across_x(buf, held, base):
        return remote(buf.at[f, :, x_other], held.at[f], base, x_dev)

    def across_core(held, base):
        return remote(held.at[f], held.at[f], base + 1, core_dev)

    def rows_x(buf, held, base, k):
        return remote(
            buf.at[f_y, part_rows(k), x_other], held.at[f_y, part_rows(k)], base + 2 + k, x_dev
        )

    def rows_core(held, base, k):
        piece = held.at[f_y, part_rows(k)]
        return remote(piece, piece, base + 2 + n_rows + k, core_dev)

    def hold_own(buf, held, base):
        across_x(buf, held, base).wait_recv()
        across_core(held, base).start()

    def hold_rows(buf, held, base):
        def step(k, carry):
            rows_x(buf, held, base, k).wait_recv()
            rows_core(held, base, k).start()
            return carry

        lax.fori_loop(0, n_rows, step, 0)

    def rows_core_done(held, base):
        for k in range(n_rows):
            rows_core(held, base, k).wait_recv()

    kv = 2 * head
    slice_width = width // n_dp
    pair_rows = pl.ds(pl.multiple_of((1 - y) * 2 * kv, 64), 2 * kv)
    sem_w_core, sem_w_y, sem_w_z, sem_w_x = take(1), take(2), take(n_hi), take(n_hi)

    def head_rows_of(t):
        return pl.ds(pl.multiple_of(t * kv, 64), kv)

    def slice_cols(d, at=0):
        return pl.ds(pl.multiple_of(at + d * slice_width, 128), slice_width)

    def w_y(dev, f_to, i, sender=c):
        return remote(
            wkv.at[:, slice_cols(dp, f_to * width)],
            w_own.at[head_rows_of(f), slice_cols(dp)],
            sem_w_y + i,
            dev,
            sem_w_y + sender,
        )

    def w_core():
        return remote(
            wkv.at[:, block_cols(f_c)], w_own.at[head_rows_of(f)], sem_w_core, core_dev
        )

    def w_z(i):
        piece = w_own.at[pair_rows, slice_cols(dp)]
        return remote(piece, piece, sem_w_z + i, far_dev(i))

    def w_x(i):
        piece = w_own.at[pair_rows, slice_cols(lax.rem(z + i, n_hi) * 2 + x)]
        return remote(piece, piece, sem_w_x + lax.rem(z + i, n_hi), x_dev)

    loads[1].wait()
    loads[2].wait()
    w_y(y_dev, f_y, 0).start()
    w_y(yc_dev, f_yc, 1).start()
    w_core().start()
    for k in range(n_rows):
        gather_y(lat_all, sem_lat, k).start()
    gather_core(lat_all, sem_lat).start()
    loads[4].wait()
    gather_core(cot_all, sem_cot).start()
    across_x(cot_all, cot_x, sem_cot_x).start()
    sums[f] = jnp.zeros(sums.shape[1:], f32)
    inners[f] = jnp.zeros(inners.shape[1:], f32)
    loads[3].wait()
    for load in small[1:]:
        load.wait()
    weigh(raw_ctx, gain_ctx, ctx_own)
    for i in range(2):
        w_y(y_dev, f_y, i, i).wait_recv()
    for i in others:
        w_z(i).start()
    w_x(0).start()
    w_own[head_rows_of(f), :] = wkv[:, block_cols(f)]
    square_sums(raw_lat, 1)
    square_sums(raw_ctx, 0)

    peers = [core_dev, y_dev, yc_dev]
    sem_sums, sem_inner = take(3), take(3)

    def exchange(buf, base):
        return [remote(buf.at[f], buf.at[f], base + i, dev) for i, dev in enumerate(peers)]

    sums_out = exchange(sums, sem_sums)
    for copy in sums_out:
        copy.start()

    def project(acc, values, weight, blocks, first):
        def step(i, carry):
            fb = blocks[0] + i * (blocks[1] - blocks[0])
            for m in range(2):
                half = pl.ds(m * (rows // 2), rows // 2)
                product = nn(values[fb, half, :], weight[block_cols(fb), :])
                if first:
                    @pl.when(i == 0)
                    def _():
                        acc[half, :] = product

                    @pl.when(i > 0)
                    def _():
                        acc[half, :] += product
                else:
                    acc[half, :] += product
            return carry

        lax.fori_loop(0, 2, step, 0)

    def project_pair(blocks, first):
        latent_cols = pl.ds(rows, rows)
        for i, fb in enumerate(blocks):
            product = nt(wkv[:, block_cols(fb)], lat_all[fb])
            if first and i == 0:
                kv_acc[0:kv, latent_cols] = product
            else:
                kv_acc[0:kv, latent_cols] += product

    mine, theirs = (f, f_c), (f_y, f_yc)
    loads[5].wait()
    loads[6].wait()
    gather_core(lat_all, sem_lat).wait_recv()
    project(acc_q, lat_all, wq, mine, True)
    project_pair(mine, True)
    for i in others:
        w_z(n_hi - i).wait_recv()
        w_x(i).start()
    w_core().wait_recv()
    pl.when(urgent)(lambda: across_x(lat_all, lat_x, sem_lat_x).start())
    for i in range(n_hi):
        w_x(i).wait_recv()

    sem_kv_core, sem_kv_y = take(2), take(1)

    def kv_core_copy(j):
        return remote(kv_send.at[j], kv_core.at[j], sem_kv_core + j, core_dev)

    def kv_y_copy():
        return remote(kv_core.at[0], kv_y, sem_kv_y, y_dev)

    patches = pl.ds(0, rows)
    for n in range(2):
        half = slice(n * (rows // 2), (n + 1) * (rows // 2))
        kv_acc[:, half] = nt(w_own[...], ctx_own[half, :])
    for j, t in enumerate((f_yc, f_c)):
        kv_send[j] = kv_acc[head_rows_of(t), patches].astype(bf16)
        kv_core_copy(j).start()
    kv_core_copy(0).wait_recv()
    kv_core[0] = (kv_acc[head_rows_of(f_y), patches] + kv_core[0].astype(f32)).astype(bf16)
    kv_y_copy().start()

    def cot_across_y():
        for k in range(n_rows):
            gather_y(cot_all, sem_cot, k).start()

    pl.when(urgent)(cot_across_y)

    pl.when(urgent)(lambda: pass_on(lat_all, sem_lat, lat_x, sem_lat_x))
    pl.when(patient)(lambda: pass_on(lat_all, sem_lat))
    wait_on(lat_all, sem_lat)
    project(acc_q, lat_all, wq, theirs, False)
    project_pair(theirs, False)

    for copy in sums_out:
        copy.wait()
    total = sums[0] + sums[1] + sums[2] + sums[3]
    scale_row[...] = lax.rsqrt(total / model_width + epsilon)

    def split_heads(across, p, by_rows, by_cols, factor):
        for h in range(heads):
            one = across[h * head : (h + 1) * head, :]
            at = pl.ds(h * ROWS, ROWS)
            by_cols[p, :, at] = one.astype(bf16)
            by_rows[p, at, :] = (one * factor).T.astype(bf16)

    def kv_by_rows(first):
        for n in range(first, first + n_rows):
            k_rows[part_rows(n), :] = flip(kv_t[0:head, part_rows(n)])
            v_rows[part_rows(n), :] = flip(kv_t[head:, part_rows(n)])

    for k in range(n_rows):
        across = acc_q[part_rows(k), :].T * scale_row[1:2, part_rows(k)]
        split_heads(across, k, q_rows, q_cols, score_scale * LOG2_E)
    kv_t[:, rows:] = (kv_acc[0:kv, rows:] * scale_row[1:2, :]).astype(bf16)
    kv_by_rows(n_rows)
    kv_core_copy(1).wait_recv()
    kv_y_copy().wait_recv()
    summed = kv_acc[head_rows_of(f), patches] + kv_core[1].astype(f32) + kv_y[...].astype(f32)
    kv_t[:, 0:rows] = (summed * scale_row[0:1, :]).astype(bf16)
    kv_by_rows(0)

    patch = lax.broadcasted_iota(jnp.int32, (1, rows), 1)
    image = jnp.zeros((1, rows), jnp.int32)
    end = jnp.int32(0)
    for i in range(lengths.shape[1]):
        end = end + lengths[0, i]
        image = image + (patch >= end).astype(jnp.int32)
    image = jnp.where(flags[...] == 1, image, -1)
    per_part = ROWS // LAT
    row_image = lax.broadcasted_iota(jnp.int32, (ROWS, 1), 0) // LAT
    col_image = lax.broadcasted_iota(jnp.int32, (1, ROWS), 1) // LAT
    same = row_image == col_image
    keys, vals = pl.ds(0, head), pl.ds(head, head)
    def own_latents(p):
        return pl.ds(pl.multiple_of(rows + p * ROWS, ROWS), ROWS)


    def head_part(h):
        return slice(h * ROWS, (h + 1) * ROWS)

    def att_x_copy(p):
        cols = part_rows(p)
        return remote(att_t.at[:, cols], att_xt.at[:, cols], sem_att_x + p, x_dev)

    def sgq_x_copy(p):
        cols = part_rows(p)
        return remote(sgq_t.at[:, cols], sgq_xt.at[:, cols], sem_sgq_x + p, x_dev)

    def forward_step(p, carry):
        far_s[...] = nn(q_rows[p], kv_t[keys, patches])
        near_s[...] = nn(q_rows[p], kv_t[keys, own_latents(p)])
        allowed = (row_image + p * per_part) == image
        for h in range(heads):
            far = jnp.where(allowed, far_s[head_part(h), :], masked_value)
            near = jnp.where(same, near_s[head_part(h), :], masked_value)
            top = jnp.maximum(
                jnp.max(far, axis=1, keepdims=True), jnp.max(near, axis=1, keepdims=True)
            )
            far, near = jnp.exp2(far - top), jnp.exp2(near - top)
            total = jnp.sum(far, axis=1, keepdims=True) + jnp.sum(near, axis=1, keepdims=True)
            inverse = 1.0 / total
            probs_c[p, head_part(h), :] = (far * inverse).astype(bf16)
            probs_l[p, head_part(h), :] = (near * inverse).astype(bf16)
        blended = nn(probs_c[p], v_rows[patches, :]) + nn(probs_l[p], v_rows[own_latents(p), :])
        for h in range(heads):
            one = blended[head_part(h), :]
            att_t[h * head : (h + 1) * head, part_rows(p)] = one.T.astype(bf16)
        att_x_copy(p).start()
        return carry

    lax.fori_loop(0, n_rows, forward_step, 0)
    def chunk_out(zt):
        return nn(att_t[...], cot_all[zt, :, x_mine]) + nn(att_xt[...], cot_x[zt])

    def chunk_query(zt):
        return nn(sgq_t[...], lat_all[zt, :, x_mine]) + nn(sgq_xt[...], lat_x[zt])

    def chunk_pair(xt):
        cols = pl.ds(pl.multiple_of(xt * feat, 128), feat)
        return nn(sgkv_all[:, patches], ctx_own[:, cols]) + nn(
            sgkv_all[:, pl.ds(rows, rows)], lat_all[f, :, cols]
        )

    class Spread:
        def __init__(self, chunk, send, recv):
            self.chunk, self.send, self.recv, self.sem = chunk, send, recv, take(3)

        def copy(self, j, dev):
            return remote(self.send.at[j], self.recv.at[j], self.sem + j, dev)

        def first(self, j):
            zt = z_1 + j * (z_2 - z)
            self.send[j] = self.chunk(zt).astype(bf16)
            self.copy(j, z1_dev).start()

        def second(self):
            value = self.chunk(z_2)
            self.copy(1, z1_dev).wait_recv()
            self.send[2] = (value + self.recv[1].astype(f32)).astype(bf16)
            self.copy(2, z2_dev).start()

        def final(self):
            dp_acc[...] = self.chunk(z)
            self.copy(0, z1_dev).wait_recv()
            self.copy(2, z2_dev).wait_recv()
            dp_acc[...] += self.recv[0].astype(f32) + self.recv[2].astype(f32)

        def wait_sends(self):
            for j in range(3):
                self.copy(j, z1_dev).wait_send()

    grad_o = Spread(chunk_out, z_send_o, z_recv_o)
    grad_q = Spread(chunk_query, z_send_q, z_recv_q)

    sem_kv_x, sem_kv_z1, sem_kv_z2, sem_kv_own = take(4), take(4), take(4), take(6)
    pair_acc = kv_acc.at[:, pl.ds(0, feat)]
    passes = lax.rem(z + f, 2) == 1

    def head_rows_at(t):
        return pl.ds(t * kv, kv)

    def pair_x_copy(t):
        at = head_rows_at(t)
        return remote(x_send_kv.at[at], x_recv_kv.at[at], sem_kv_x + t, x_dev)

    def pair_z_copy(t):
        at = head_rows_at(t)
        return remote(x_recv_kv.at[at], z_recv_kv.at[at], sem_kv_z1 + t, z1_dev)

    def pair_far_copy(t):
        at = head_rows_at(t)
        dev = (z_2 * 2 + x, t)
        return remote(x_recv_kv.at[at], own_recv.at[1], sem_kv_z2 + t, dev, sem_kv_own + 5)

    def pair_own_copy(t):
        return remote(
            own_send.at[t], own_recv.at[0], sem_kv_own + t, (dp, t), sem_kv_own + 4
        )

    def pair_first():
        x_send_kv[...] = chunk_pair(1 - x).astype(bf16)
        for t in range(4):
            pair_x_copy(t).start()
        pair_acc[...] = chunk_pair(x)

    def pair_step(t, i):
        at = head_rows_at(t)
        if i == 0:
            pair_x_copy(t).wait_recv()
            pair_acc[at, :] += x_recv_kv[at, :].astype(f32)

            @pl.when(passes)
            def _():
                x_recv_kv[at, :] = pair_acc[at, :].astype(bf16)
                pair_z_copy(t).start()

            return

        @pl.when(jnp.logical_not(passes))
        def _():
            pair_z_copy(t).wait_recv()
            pair_acc[at, :] += z_recv_kv[at, :].astype(f32)

        @pl.when(middle)
        def _():
            x_recv_kv[at, :] = pair_acc[at, :].astype(bf16)
            pair_far_copy(t).start()

        @pl.when((z == f) & (f != t))
        def _():
            own_send[t] = pair_acc[at, :].astype(bf16)
            pair_own_copy(t).start()

    def pair_result():
        pair_far_copy(0).wait_recv()
        far = own_recv[1].astype(f32)
        at = pl.ds(feat, feat)

        @pl.when(z == f)
        def _():
            kv_acc[0:kv, at] = kv_acc[head_rows_of(f), pl.ds(0, feat)] + far

        @pl.when(z != f)
        def _():
            pair_own_copy(0).wait_recv()
            kv_acc[0:kv, at] = own_recv[0].astype(f32) + far

    def pair_sends_done():
        for t in range(4):
            pair_x_copy(t).wait_send()
            pl.when(passes)(lambda t=t: pair_z_copy(t).wait_send())
            pl.when(middle)(lambda t=t: pair_far_copy(t).wait_send())

        @pl.when(z == f)
        def _():
            for t in range(4):
                pl.when(f != t)(lambda t=t: pair_own_copy(t).wait_send())

    class Collect:
        def __init__(self, part, index, seen=None):
            self.part, self.index, self.sem = part, index, take(3 * n_cols)
            self.seen = seen

        def core_copy(self, j, k):
            return remote(
                core_send.at[j, :, part_cols(k)],
                core_recv.at[self.index, j, :, part_cols(k)],
                self.sem + j * n_cols + k,
                core_dev,
            )

        def y_copy(self, k):
            return remote(
                core_recv.at[self.index, 0, :, part_cols(k)],
                y_recv.at[self.index, :, part_cols(k)],
                self.sem + 2 * n_cols + k,
                y_dev,
            )

        def product(self, fb, k):
            value = self.part(fb, k)
            if self.seen is not None:
                self.seen(fb, k, value)
            return value

        def send_core(self):
            def core_step(n, carry):
                j, k = n // n_cols, lax.rem(n, n_cols)
                fb = jnp.where(j == 0, f_yc, f_c)
                core_send[j, :, part_cols(k)] = self.product(fb, k).astype(bf16)
                self.core_copy(j, k).start()
                return carry

            lax.fori_loop(0, 2 * n_cols, core_step, 0)

        def send_y(self, first, last, start=True):
            def y_step(k, carry):
                value = self.product(f_y, k)
                self.core_copy(0, k).wait_recv()
                value = value + core_recv[self.index, 0, :, part_cols(k)].astype(f32)
                core_recv[self.index, 0, :, part_cols(k)] = value.astype(bf16)
                if start:
                    self.y_copy(k).start()
                return carry

            lax.fori_loop(first, last, y_step, 0)

        def core_sends_done(self):
            for j in range(2):
                for k in range(n_cols):
                    self.core_copy(j, k).wait_send()

        def total(self, k):
            value = self.part(f, k)
            self.core_copy(1, k).wait_recv()
            self.y_copy(k).wait_recv()
            return (
                value
                + core_recv[self.index, 1, :, part_cols(k)].astype(f32)
                + y_recv[self.index, :, part_cols(k)].astype(f32)
            )

        def wait_y_sends(self):
            for k in range(n_cols):
                self.y_copy(k).wait_send()

    def gain_add(index, k, value, weighed):
        products = (value * weighed.astype(f32)).reshape(rows // 8, 8, piece)
        gain_part[index, :, part_cols(k)] += jnp.sum(products, axis=0)

    def part_branch(fb, k):
        return nt(att[...], wo[cols_at(fb, k), :])

    def part_lat(fb, k):
        return nt(sgq[...], wq[cols_at(fb, k), :])

    def seen_lat(fb, k, value):
        gain_add(4 + fb, k, value, lat_all[fb, :, part_cols(k)])

    branch = Collect(part_branch, 0)
    back_lat = Collect(part_lat, 1, seen_lat)
    gain_part[...] = jnp.zeros(gain_part.shape, f32)

    gather_core(cot_all, sem_cot).wait_recv()
    project(acc_q, cot_all, wo, mine, True)
    for k in range(n_rows):
        att[part_rows(k), :] = flip(att_t[:, part_rows(k)])
    pl.when(patient)(cot_across_y)
    branch.send_core()

    hold_own(cot_all, cot_x, sem_cot_x)
    pl.when(urgent)(lambda: hold_own(lat_all, lat_x, sem_lat_x))
    across_core(cot_x, sem_cot_x).wait_recv()
    for p in range(n_rows):
        att_x_copy(p).wait_recv()
    near_j = jnp.where(z // 2 == y, 0, 1)
    grad_o.first(near_j)

    @pl.when(urgent)
    def _():
        pass_on(cot_all, sem_cot, cot_x, sem_cot_x)
        hold_rows(lat_all, lat_x, sem_lat_x)

    pl.when(patient)(lambda: wait_on(cot_all, sem_cot))

    gkv[:, patches] = jnp.zeros((kv, rows), f32)

    def backward_step(p, carry):
        far_s[...] = nn(ga_rows[p], kv_t[vals, patches])
        near_s[...] = nn(ga_rows[p], kv_t[vals, own_latents(p)])
        for h in range(heads):
            far_p = probs_c[p, head_part(h), :].astype(f32)
            near_p = probs_l[p, head_part(h), :].astype(f32)
            far_d, near_d = far_s[head_part(h), :], near_s[head_part(h), :]
            inner = jnp.sum(far_p * far_d, axis=1, keepdims=True) + jnp.sum(
                near_p * near_d, axis=1, keepdims=True
            )
            far_g[head_part(h), :] = (far_p * (far_d - inner)).astype(bf16)
            near_g[head_part(h), :] = (near_p * (near_d - inner)).astype(bf16)
        grad_query = nn(far_g[...], k_rows[patches, :]) + nn(near_g[...], k_rows[own_latents(p), :])
        total = jnp.zeros((1, ROWS), f32)
        for h in range(heads):
            one = grad_query[head_part(h), :].T * score_scale
            query = q_cols[p, :, head_part(h)].astype(f32)
            total = total + jnp.sum(one * query, axis=0, keepdims=True)
            sgq_t[h * head : (h + 1) * head, part_rows(p)] = (
                one * scale_row[1:2, part_rows(p)]
            ).astype(bf16)
        inners[f, 1:2, part_rows(p)] = total
        sgq_x_copy(p).start()
        gkv[keys, patches] += nn(q_cols[p], far_g[...])
        gkv[keys, own_latents(p)] = nn(q_cols[p], near_g[...])
        gkv[vals, patches] += nn(ga_cols[p], probs_c[p])
        gkv[vals, own_latents(p)] = nn(ga_cols[p], probs_l[p])
        return carry

    def cot_step(p, carry):
        @pl.when(patient)
        def _():
            gather_y(cot_all, sem_cot, p).wait_recv()
            gather_on(cot_all, sem_cot, p).start()

        pl.when(urgent)(lambda: gather_on(cot_all, sem_cot, p).wait_recv())
        value = acc_q[part_rows(p), :]
        for fb in (f_y, f_yc):
            value = value + nn(cot_all[fb, part_rows(p), :], wo[block_cols(fb), :])
        split_heads(value.T, p, ga_rows, ga_cols, 1.0)
        return backward_step(p, carry)

    lax.fori_loop(0, n_rows // 2, cot_step, 0)
    pl.when(urgent)(lambda: hold_rows(cot_all, cot_x, sem_cot_x))
    pl.when(patient)(lambda: rows_core_done(cot_x, sem_cot_x))
    grad_o.first(1 - near_j)
    early = z // 2 != y
    pl.when(early)(grad_o.second)
    branch.send_y(0, 1)
    lax.fori_loop(n_rows // 2, n_rows, cot_step, 0)
    gkv[keys, :] = gkv[keys, :] * score_scale
    products = jnp.sum(gkv[...] * kv_t[...].astype(f32), axis=0, keepdims=True)
    inners[f, 0:1, :] = products[:, 0:rows]
    inners[f, 1:2, :] += products[:, rows:]
    inner_out = exchange(inners, sem_inner)
    for copy in inner_out:
        copy.start()
    sgkv_all[head_rows_of(f), 0:rows] = (gkv[:, 0:rows] * scale_row[0:1, :]).astype(bf16)
    sgkv_all[head_rows_of(f), rows:] = (gkv[:, rows:] * scale_row[1:2, :]).astype(bf16)
    sem_gkv = take(3)

    def gkv_copy(t, i, dev):
        piece = sgkv_all.at[head_rows_of(t)]
        return remote(piece, piece, sem_gkv + i, dev)

    gkv_copy(f, 0, y_dev).start()
    gkv_copy(f, 1, core_dev).start()
    for k in range(n_rows):
        sgq[part_rows(k), :] = flip(sgq_t[:, part_rows(k)])

    late = jnp.logical_not(early)

    def all_rows_x(buf, held, base):
        for k in range(n_rows):
            rows_x(buf, held, base, k).start()

    pl.when(patient & early)(lambda: across_x(lat_all, lat_x, sem_lat_x).start())

    @pl.when(patient & late)
    def _():
        all_rows_x(cot_all, cot_x, sem_cot_x)
        all_rows_x(lat_all, lat_x, sem_lat_x)

    @pl.when(patient)
    def _():
        across_core(lat_x, sem_lat_x).wait_recv()
        rows_core_done(lat_x, sem_lat_x)

    for p in range(n_rows):
        sgq_x_copy(p).wait_recv()
    grad_q.first(1)
    grad_q.first(0)
    branch.send_y(1, n_cols)
    branch.core_sends_done()
    back_lat.send_core()
    gkv_copy(f, 0, y_dev).wait_recv()
    gkv_copy(f_y, 2, core_dev).start()
    gkv_copy(f, 1, core_dev).wait_recv()
    gkv_copy(f_y, 2, core_dev).wait_recv()
    pair_first()

    @pl.when(patient & early)
    def _():
        all_rows_x(cot_all, cot_x, sem_cot_x)
        all_rows_x(lat_all, lat_x, sem_lat_x)

    pl.when(patient & late)(lambda: across_x(lat_all, lat_x, sem_lat_x).start())

    def patient_own_lat():
        pl.when(patient)(lambda: hold_own(lat_all, lat_x, sem_lat_x))
        pl.when(urgent)(lambda: across_core(lat_x, sem_lat_x).wait_recv())

    def patient_rows(buf, held, base):
        pl.when(patient)(lambda: hold_rows(buf, held, base))
        pl.when(urgent)(lambda: rows_core_done(held, base))

    @pl.when(early)
    def _():
        patient_own_lat()
        grad_q.second()

    @pl.when(late)
    def _():
        patient_rows(cot_all, cot_x, sem_cot_x)
        grad_o.second()

    back_lat.send_y(0, n_cols, False)
    outs = []

    def put(src, dst, i):
        copy = local_copy(src, dst, i)
        copy.start()
        outs.append(copy)

    for copy in inner_out:
        copy.wait()
    coef_row[...] = (
        scale_row[...]
        * scale_row[...]
        * (inners[0] + inners[1] + inners[2] + inners[3])
        / model_width
    )

    coef_cols = coef_row[...].T
    back_lat.core_sends_done()
    for k in range(n_rows):
        sgc[part_rows(k), :] = flip(sgkv_all[:, part_rows(k)])
        sgl[part_rows(k), :] = flip(sgkv_all[:, part_rows(n_rows + k)])

    def finish_ctx(k, carry):
        value = nn(sgc[...], w_own[:, part_cols(k)])
        gain_add(f, k, value, ctx_own[:, part_cols(k)])
        value = value * gain_ctx[:, cols_at(f, k)]
        value = value - raw_ctx[:, part_cols(k)].astype(f32) * coef_cols[:, 0:1]
        core_send[0, :, part_cols(k)] = value.astype(bf16)
        return carry

    lax.fori_loop(0, n_cols, finish_ctx, 0)
    put(core_send.at[0], out_context, 10)
    pair_step(0, 0)

    def gain_own(k, carry):
        value = part_lat(f, k) + nn(sgl[...], w_own[:, part_cols(k)])
        gain_add(4 + f, k, value, lat_all[f, :, part_cols(k)])
        return carry

    lax.fori_loop(0, n_cols, gain_own, 0)
    for i in range(4):
        gain_all[f, i : i + 1, :] = (
            jnp.sum(gain_part[i], axis=0, keepdims=True) / gain_ctx[:, block_cols(i)]
        )
        gain_all[f, 4 + i : 5 + i, :] = (
            jnp.sum(gain_part[4 + i], axis=0, keepdims=True) / gain_lat[:, block_cols(i)]
        )
    sem_gain, sem_gain_sum = take(2 * n_hi), take(3)
    gain_peers = exchange(gain_all, sem_gain_sum)
    for copy in gain_peers:
        copy.start()
    for k in range(n_cols):
        back_lat.y_copy(k).start()
    part = width // n_dp

    def dp_cols(d, n):
        return pl.ds(pl.multiple_of(d * part, 128), n * part)

    gain_targets = [(i, lax.rem(z + i, n_hi) * 2 + x, far_dev(i)) for i in others]
    gain_targets += [(n_hi, z * 2 + 1 - x, x_dev)]
    gain_targets += [(n_hi + i, lax.rem(z + i, n_hi) * 2 + 1 - x, far_x_dev(i)) for i in others]
    gain_copies = [
        remote(gain_sum.at[:, dp_cols(d, 1)], gain_recv.at[i], sem_gain + i, dev)
        for i, d, dev in gain_targets
    ]
    pair_step(1, 0)

    @pl.when(late)
    def _():
        patient_rows(lat_all, lat_x, sem_lat_x)
        grad_q.second()

    pair_step(2, 0)
    def finish(k, carry):
        value = raw_lat[:, part_cols(k)].astype(f32) + branch.total(k)
        y_recv[0, :, part_cols(k)] = value.astype(bf16)
        return carry

    def finish_lat(k):
        value = back_lat.total(k) + nn(sgl[...], w_own[:, part_cols(k)])
        value = value * gain_lat[:, cols_at(f, k)]
        value = value - raw_lat[:, part_cols(k)].astype(f32) * coef_cols[:, 1:2]
        value = value + cot_all[f, :, part_cols(k)].astype(f32)
        y_recv[1, :, part_cols(k)] = value.astype(bf16)
        put(y_recv.at[1, :, part_cols(k)], out_grad_lat.at[:, part_cols(k)], 20 + k)

    def put_weight(spread, at, out, i):
        spread.final()
        at[...] = dp_acc[...].T
        put(at, out, i)

    out_copy = local_copy(acc_q, out_out, 6)
    outs.append(out_copy)

    def finish_out():
        grad_o.final()
        acc_q[...] = dp_acc[...].T
        out_copy.start()

    for copy in gain_peers:
        copy.wait()
    gain_sum[...] = gain_all[0] + gain_all[1] + gain_all[2] + gain_all[3]
    for copy in gain_copies:
        copy.start()
    pair_step(3, 0)
    lax.fori_loop(0, n_cols, finish, 0)
    put(y_recv.at[0], out_latents, 9)
    pl.when(late)(finish_out)
    finish_lat(0)
    pair_step(0, 1)
    pair_step(1, 1)
    finish_lat(1)
    pair_step(2, 1)

    pair_step(3, 1)

    @pl.when(early)
    def _():
        patient_rows(cot_all, cot_x, sem_cot_x)
        finish_out()

    for buf, base in ((lat_all, sem_lat), (cot_all, sem_cot)):
        gather_done(buf, base)
    branch.wait_y_sends()
    for p in range(n_rows):
        att_x_copy(p).wait_send()
        sgq_x_copy(p).wait_send()
    w_core().wait_send()
    for i in range(2):
        w_y(y_dev, f_y, i).wait_send()
    for i in others:
        w_z(i).wait_send()
    for i in range(n_hi):
        w_x(i).wait_send()
    for j in range(2):
        kv_core_copy(j).wait_send()
    kv_y_copy().wait_send()
    for i in range(3):
        gkv_copy(f, i, core_dev).wait_send()
    pl.when(early)(lambda: patient_rows(lat_all, lat_x, sem_lat_x))
    pl.when(late)(patient_own_lat)
    finish_lat(2)
    put_weight(grad_q, far_s.at[:, pl.ds(0, heads * head)], out_query, 7)
    finish_lat(3)
    pair_result()
    for i, out in enumerate((out_key, out_value)):
        put(kv_acc.at[pl.ds(i * head, head), pl.ds(feat, feat)], out, 8 + 5 * i)
    mine_all = gain_sum[:, dp_cols(dp, 1)]
    for copy in gain_copies:
        copy.wait()
    for i, _, _ in gain_targets:
        mine_all = mine_all + gain_recv[i]
    index = lax.broadcasted_iota(jnp.int32, mine_all.shape, 0)
    gain_out[0] = jnp.sum(jnp.where(index == f, mine_all, 0.0), axis=0, keepdims=True)
    gain_out[1] = jnp.sum(jnp.where(index == 4 + f, mine_all, 0.0), axis=0, keepdims=True)
    put(gain_out.at[0], out_gain_c, 2)
    put(gain_out.at[1], out_gain_l, 14)
    for copy in outs:
        copy.wait()
    back_lat.wait_y_sends()
    for spread in (grad_o, grad_q):
        spread.wait_sends()
    for buf, held, base in ((lat_all, lat_x, sem_lat_x), (cot_all, cot_x, sem_cot_x)):
        across_x(buf, held, base).wait_send()
        across_core(held, base).wait_send()
        for k in range(n_rows):
            rows_x(buf, held, base, k).wait_send()
            rows_core(held, base, k).wait_send()
    pair_sends_done()


def hand_on(*refs):
    n = (len(refs) - 2) // 3
    ins, outs, held, sem_in, sem_out = refs[:n], refs[n : 2 * n], refs[2 * n : 3 * n], *refs[3 * n :]
    take_in = [pltpu.make_async_copy(ins[i], held[i], sem_in.at[i]) for i in range(n)]
    give_out = [pltpu.make_async_copy(held[i], outs[i], sem_out.at[i]) for i in range(n)]
    for copy in take_in:
        copy.start()
    for i in range(n):
        take_in[i].wait()
        give_out[i].start()
    for copy in give_out:
        copy.wait()


def kernel_local(
    n_dp,
    context,
    latents,
    gain_ctx,
    gain_lat,
    w_query,
    key_matrix,
    value_matrix,
    w_out,
    lengths,
    patch_flags,
    cotangent,
):
    rows, width = context.shape
    model_width = gain_ctx.shape[0]
    units = w_query.shape[1]
    kv = 2 * key_matrix.shape[1]
    heads = units // HEAD_DIM
    n_hi = n_dp // 2
    feat = model_width // n_dp
    any_space = pl.BlockSpec(memory_space=pl.ANY)
    block = jax.ShapeDtypeStruct((rows, width), bf16)
    shaped = jax.ShapeDtypeStruct
    out = pl.pallas_call(
        functools.partial(block_kernel, n_dp),
        out_shape=(
            block,
            block,
            block,
            shaped((feat, units), f32),
            shaped((kv // 2, feat), f32),
            shaped((kv // 2, feat), f32),
            shaped((feat, units), f32),
            shaped((1, width // n_dp), f32),
            shaped((1, width // n_dp), f32),
        ),
        in_specs=[any_space] * 11,
        out_specs=(any_space,) * 9,
        scratch_shapes=[
            pltpu.VMEM((1, model_width), f32),
            pltpu.VMEM((1, model_width), f32),
            pltpu.SMEM(lengths.shape, jnp.int32),
            pltpu.VMEM((1, rows), jnp.int32),
            pltpu.VMEM((2, 1, width // n_dp), f32),
            pltpu.VMEM((4, rows, width), bf16),
            pltpu.VMEM((4, rows, width), bf16),
            pltpu.VMEM((rows, width), bf16),
            pltpu.VMEM((rows, width), bf16),
            pltpu.VMEM((rows, width), bf16),
            pltpu.VMEM((model_width, units), bf16),
            pltpu.VMEM((kv, model_width), bf16),
            pltpu.VMEM((4 * kv, width), bf16),
            pltpu.VMEM((model_width, units), bf16),
            pltpu.VMEM((rows, units), f32),
            pltpu.VMEM((4 * kv, 2 * rows), f32),
            pltpu.VMEM((units, rows), bf16),
            pltpu.VMEM((units, rows), bf16),
            pltpu.VMEM((rows // ROWS, heads * ROWS, HEAD_DIM), bf16),
            pltpu.VMEM((rows // ROWS, HEAD_DIM, heads * ROWS), bf16),
            pltpu.VMEM((rows // ROWS, heads * ROWS, HEAD_DIM), bf16),
            pltpu.VMEM((rows // ROWS, HEAD_DIM, heads * ROWS), bf16),
            pltpu.VMEM((2 * rows, HEAD_DIM), bf16),
            pltpu.VMEM((2 * rows, HEAD_DIM), bf16),
            pltpu.VMEM((heads * ROWS, rows), f32),
            pltpu.VMEM((heads * ROWS, ROWS), f32),
            pltpu.VMEM((heads * ROWS, rows), bf16),
            pltpu.VMEM((heads * ROWS, ROWS), bf16),
            pltpu.VMEM((rows, units), bf16),
            pltpu.VMEM((rows, units), bf16),
            pltpu.VMEM((kv, 2 * rows), bf16),
            pltpu.VMEM((2, kv, rows), bf16),
            pltpu.VMEM((2, kv, rows), bf16),
            pltpu.VMEM((kv, rows), bf16),
            pltpu.VMEM((rows // ROWS, heads * ROWS, rows), bf16),
            pltpu.VMEM((rows // ROWS, heads * ROWS, ROWS), bf16),
            pltpu.VMEM((kv, 2 * rows), f32),
            pltpu.VMEM((4 * kv, 2 * rows), bf16),
            pltpu.VMEM((rows, 4 * kv), bf16),
            pltpu.VMEM((rows, 4 * kv), bf16),
            pltpu.VMEM((4, 8, rows), f32),
            pltpu.VMEM((4, 8, rows), f32),
            pltpu.VMEM((8, rows), f32),
            pltpu.VMEM((8, rows), f32),
            pltpu.VMEM((8, 8, width), f32),
            pltpu.VMEM((8, width), f32),
            pltpu.VMEM((2 * n_hi, 8, width // n_dp), f32),
            pltpu.VMEM((4, 8, width), f32),
            pltpu.VMEM((2, rows, width), bf16),
            pltpu.VMEM((2, 2, rows, width), bf16),
            pltpu.VMEM((2, rows, width), bf16),
            pltpu.VMEM((4, rows, feat), bf16),
            pltpu.VMEM((4, rows, feat), bf16),
            pltpu.VMEM((units, rows), bf16),
            pltpu.VMEM((units, rows), bf16),
            pltpu.VMEM((3, units, feat), bf16),
            pltpu.VMEM((3, units, feat), bf16),
            pltpu.VMEM((3, units, feat), bf16),
            pltpu.VMEM((3, units, feat), bf16),
            pltpu.VMEM((4 * kv, feat), bf16),
            pltpu.VMEM((4 * kv, feat), bf16),
            pltpu.VMEM((4 * kv, feat), bf16),
            pltpu.VMEM((4, kv, feat), bf16),
            pltpu.VMEM((2, kv, feat), bf16),
            pltpu.VMEM((units, feat), f32),
            pltpu.SemaphoreType.DMA((160,)),
            pltpu.SemaphoreType.DMA((160,)),
            pltpu.SemaphoreType.DMA((24,)),
        ],
        compiler_params=pltpu.CompilerParams(
            collective_id=0, has_side_effects=True, vmem_limit_bytes=64 << 20
        ),
        name="block",
    )(
        context,
        latents,
        cotangent,
        gain_ctx.reshape(1, model_width),
        gain_lat.reshape(1, model_width),
        w_query,
        key_matrix.T,
        value_matrix.T,
        w_out,
        lengths,
        patch_flags.reshape(1, rows),
    )
    out = pl.pallas_call(
        hand_on,
        out_shape=tuple(shaped(a.shape, a.dtype) for a in out),
        in_specs=[any_space] * 9,
        out_specs=(any_space,) * 9,
        scratch_shapes=[pltpu.VMEM(a.shape, a.dtype) for a in out]
        + [pltpu.SemaphoreType.DMA((9,)), pltpu.SemaphoreType.DMA((9,))],
        compiler_params=pltpu.CompilerParams(vmem_limit_bytes=64 << 20),
        name="hand_on",
    )(*out)
    latents_out, grad_context, grad_latents, g_query, g_key, g_value, g_out, gain_c, gain_l = out
    return (
        latents_out,
        grad_context,
        grad_latents,
        g_query,
        g_key.T,
        g_value.T,
        g_out,
        gain_c,
        gain_l,
    )


def solution(mesh):
    n_dp = mesh.shape["dp"]
    body = functools.partial(kernel_local, n_dp) if n_dp == 8 else plain_local
    return jax.shard_map(
        body,
        mesh=mesh,
        in_specs=(
            P("dp", "tensor"),
            P("dp", "tensor"),
            P(),
            P(),
            P(None, "tensor"),
            P(None, "tensor"),
            P(None, "tensor"),
            P(None, "tensor"),
            P("dp", None),
            P("dp"),
            P("dp", "tensor"),
        ),
        out_specs=(
            P("dp", "tensor"),
            P("dp", "tensor"),
            P("dp", "tensor"),
            P("dp", "tensor"),
            P("dp", "tensor"),
            P("dp", "tensor"),
            P("dp", "tensor"),
            P("tensor", "dp"),
            P("tensor", "dp"),
        ),
        check_vma=False,
    )
```

profile of v0, /device:TPU:7, one launch (start us, length us, event | category | flops | bytes accessed | tf_op | source)
XLA Modules:
  0.0 133.7 jit_solution(8378139060216000422)
XLA Ops:
  0.6 128.7 %block.1 = (bf16[512,1024]{1,0:T(8,128)(2,1)}, bf16[512,1024]{1,0:T(8,128)(2,1)}, bf16[512,1024]{1,0:T(8,128)(2,1)}, f32[512,384]{1,0:T(8,128)}, f32[96,512]{1,0...) custom-call(bf16[512,1024]{1,0:T(8,128)(2,1)} %context.1, ...), custom_call_target="tpu_custom_call" | custom-call | tf_op jit(solution)/shard_map/block/pallas_call | solution.py:1325
  129.3 4.2 %hand_on.1 = (bf16[512,1024]{1,0:T(8,128)(2,1)}, bf16[512,1024]{1,0:T(8,128)(2,1)}, bf16[512,1024]{1,0:T(8,128)(2,1)}, f32[512,384]{1,0:T(8,128)}, f32[96,512]{1...) custom-call(bf16[512,1024]{1,0:T(8,128)(2,1)} %get-tuple-element.27.refs_0_, ...), custom_call_target="tpu_custom_call" | custom-call | tf_op jit(solution)/shard_map/hand_on/pallas_call | solution.py:1427
where the time goes:
time: 134 us
  Pallas kernels  133 us (99%)
    pallas_call x1, Pallas kernels, kernel_local(): pl.pallas_call(functools.partial(block_kernel, n_dp), out_shape=(block, b...  129 us
    pallas_call x1, Pallas kernels, kernel_local(): pl.pallas_call(hand_on, out_shape=tuple((shaped(a.shape, a.dtype) for a i...  4.22 us

commit v1 on v0

--- a/solution.py
+++ b/solution.py
@@ -793,67 +793,78 @@
     grad_o = Spread(chunk_out, z_send_o, z_recv_o)
     grad_q = Spread(chunk_query, z_send_q, z_recv_q)
 
-    sem_kv_x, sem_kv_z1, sem_kv_z2, sem_kv_own = take(4), take(4), take(4), take(6)
+    sem_kv_x, sem_kv_z1, sem_kv_z2 = take(8), take(8), take(8)
+    sem_kv_own, sem_kv_in = take(8), take(4)
     pair_acc = kv_acc.at[:, pl.ds(0, feat)]
     passes = lax.rem(z + f, 2) == 1
 
-    def head_rows_at(t):
-        return pl.ds(t * kv, kv)
-
-    def pair_x_copy(t):
-        at = head_rows_at(t)
-        return remote(x_send_kv.at[at], x_recv_kv.at[at], sem_kv_x + t, x_dev)
-
-    def pair_z_copy(t):
-        at = head_rows_at(t)
-        return remote(x_recv_kv.at[at], z_recv_kv.at[at], sem_kv_z1 + t, z1_dev)
-
-    def pair_far_copy(t):
-        at = head_rows_at(t)
+    def piece_of(q):
+        t = lax.rem(q // 2 + 2 * (1 - y), 4)
+        return t, pl.ds(pl.multiple_of(t * kv + (q % 2) * head, 32), head)
+
+    def half_of(q):
+        return pl.ds((q % 2) * head, head)
+
+    def pair_x_copy(q):
+        _, at = piece_of(q)
+        return remote(x_send_kv.at[at], x_recv_kv.at[at], sem_kv_x + q, x_dev)
+
+    def pair_z_copy(q):
+        _, at = piece_of(q)
+        return remote(x_recv_kv.at[at], z_recv_kv.at[at], sem_kv_z1 + q, z1_dev)
+
+    def pair_far_copy(q):
+        t, at = piece_of(q)
+        to = own_recv.at[1, half_of(q)]
         dev = (z_2 * 2 + x, t)
-        return remote(x_recv_kv.at[at], own_recv.at[1], sem_kv_z2 + t, dev, sem_kv_own + 5)
-
-    def pair_own_copy(t):
-        return remote(
-            own_send.at[t], own_recv.at[0], sem_kv_own + t, (dp, t), sem_kv_own + 4
-        )
+        return remote(x_recv_kv.at[at], to, sem_kv_z2 + q, dev, sem_kv_in + 2 + q % 2)
+
+    def pair_own_copy(q):
+        t, _ = piece_of(q)
+        to = own_recv.at[0, half_of(q)]
+        return remote(own_send.at[q], to, sem_kv_own + q, (dp, t), sem_kv_in + q % 2)
 
     def pair_first():
         x_send_kv[...] = chunk_pair(1 - x).astype(bf16)
-        for t in range(4):
-            pair_x_copy(t).start()
+        for q in range(8):
+            pair_x_copy(q).start()
         pair_acc[...] = chunk_pair(x)
 
-    def pair_step(t, i):
-        at = head_rows_at(t)
+    def pair_piece(q, i):
+        t, at = piece_of(q)
         if i == 0:
-            pair_x_copy(t).wait_recv()
+            pair_x_copy(q).wait_recv()
             pair_acc[at, :] += x_recv_kv[at, :].astype(f32)
 
             @pl.when(passes)
             def _():
                 x_recv_kv[at, :] = pair_acc[at, :].astype(bf16)
-                pair_z_copy(t).start()
+                pair_z_copy(q).start()
 
             return
 
         @pl.when(jnp.logical_not(passes))
         def _():
-            pair_z_copy(t).wait_recv()
+            pair_z_copy(q).wait_recv()
             pair_acc[at, :] += z_recv_kv[at, :].astype(f32)
 
         @pl.when(middle)
         def _():
             x_recv_kv[at, :] = pair_acc[at, :].astype(bf16)
-            pair_far_copy(t).start()
+            pair_far_copy(q).start()
 
         @pl.when((z == f) & (f != t))
         def _():
-            own_send[t] = pair_acc[at, :].astype(bf16)
-            pair_own_copy(t).start()
+            own_send[q] = pair_acc[at, :].astype(bf16)
+            pair_own_copy(q).start()
+
+    def pair_step(n, i):
+        pair_piece(2 * n, i)
+        pair_piece(2 * n + 1, i)
 
     def pair_result():
-        pair_far_copy(0).wait_recv()
+        for q in range(2):
+            pair_far_copy(q).wait_recv()
         far = own_recv[1].astype(f32)
         at = pl.ds(feat, feat)
 
@@ -863,19 +874,20 @@
 
         @pl.when(z != f)
         def _():
-            pair_own_copy(0).wait_recv()
+            for q in range(2):
+                pair_own_copy(q).wait_recv()
             kv_acc[0:kv, at] = own_recv[0].astype(f32) + far
 
     def pair_sends_done():
-        for t in range(4):
-            pair_x_copy(t).wait_send()
-            pl.when(passes)(lambda t=t: pair_z_copy(t).wait_send())
-            pl.when(middle)(lambda t=t: pair_far_copy(t).wait_send())
+        for q in range(8):
+            pair_x_copy(q).wait_send()
+            pl.when(passes)(lambda q=q: pair_z_copy(q).wait_send())
+            pl.when(middle)(lambda q=q: pair_far_copy(q).wait_send())
 
         @pl.when(z == f)
         def _():
-            for t in range(4):
-                pl.when(f != t)(lambda t=t: pair_own_copy(t).wait_send())
+            for q in range(8):
+                pl.when(piece_of(q)[0] != f)(lambda q=q: pair_own_copy(q).wait_send())
 
     class Collect:
         def __init__(self, part, index, seen=None):
@@ -1033,9 +1045,10 @@
     pl.when(patient)(lambda: rows_core_done(cot_x, sem_cot_x))
     grad_o.first(1 - near_j)
     early = z // 2 != y
+    branch.send_y(0, 1)
+    lax.fori_loop(n_rows // 2, n_rows - 1, cot_step, 0)
     pl.when(early)(grad_o.second)
-    branch.send_y(0, 1)
-    lax.fori_loop(n_rows // 2, n_rows, cot_step, 0)
+    cot_step(n_rows - 1, 0)
     gkv[keys, :] = gkv[keys, :] * score_scale
     products = jnp.sum(gkv[...] * kv_t[...].astype(f32), axis=0, keepdims=True)
     inners[f, 0:1, :] = products[:, 0:rows]
@@ -1058,6 +1071,10 @@
 
     late = jnp.logical_not(early)
 
+    def patient_rows(buf, held, base):
+        pl.when(patient)(lambda: hold_rows(buf, held, base))
+        pl.when(urgent)(lambda: rows_core_done(held, base))
+
     def all_rows_x(buf, held, base):
         for k in range(n_rows):
             rows_x(buf, held, base, k).start()
@@ -1081,6 +1098,11 @@
     branch.send_y(1, n_cols)
     branch.core_sends_done()
     back_lat.send_core()
+    @pl.when(late)
+    def _():
+        patient_rows(cot_all, cot_x, sem_cot_x)
+        grad_o.second()
+
     gkv_copy(f, 0, y_dev).wait_recv()
     gkv_copy(f_y, 2, core_dev).start()
     gkv_copy(f, 1, core_dev).wait_recv()
@@ -1098,19 +1120,10 @@
         pl.when(patient)(lambda: hold_own(lat_all, lat_x, sem_lat_x))
         pl.when(urgent)(lambda: across_core(lat_x, sem_lat_x).wait_recv())
 
-    def patient_rows(buf, held, base):
-        pl.when(patient)(lambda: hold_rows(buf, held, base))
-        pl.when(urgent)(lambda: rows_core_done(held, base))
-
     @pl.when(early)
     def _():
         patient_own_lat()
         grad_q.second()
-
-    @pl.when(late)
-    def _():
-        patient_rows(cot_all, cot_x, sem_cot_x)
-        grad_o.second()
 
     back_lat.send_y(0, n_cols, False)
     outs = []
@@ -1400,7 +1413,7 @@
             pltpu.VMEM((4 * kv, feat), bf16),
             pltpu.VMEM((4 * kv, feat), bf16),
             pltpu.VMEM((4 * kv, feat), bf16),
-            pltpu.VMEM((4, kv, feat), bf16),
+            pltpu.VMEM((8, HEAD_DIM, feat), bf16),
             pltpu.VMEM((2, kv, feat), bf16),
             pltpu.VMEM((units, feat), f32),
             pltpu.SemaphoreType.DMA((160,)),

time: 134 us -> 133 us (level)
  no operation moved by 1% of the time
where the time goes in v1:
time: 133 us; the launch traced here: 132 us
  Pallas kernels  132 us (99%)
    pallas_call x1, Pallas kernels, kernel_local(): pl.pallas_call(functools.partial(block_kernel, n_dp), out_shape=(block, b...  127 us
    pallas_call x1, Pallas kernels, kernel_local(): pl.pallas_call(hand_on, out_shape=tuple((shaped(a.shape, a.dtype) for a i...  4.22 us

profile of v1, /device:TPU:7, one launch (start us, length us, event | category | flops | bytes accessed | tf_op | source)
XLA Modules:
  0.0 132.4 jit_solution(4450942651940937777)
XLA Ops:
  0.6 127.4 %block.1 = (bf16[512,1024]{1,0:T(8,128)(2,1)}, bf16[512,1024]{1,0:T(8,128)(2,1)}, bf16[512,1024]{1,0:T(8,128)(2,1)}, f32[512,384]{1,0:T(8,128)}, f32[96,512]{1,0...) custom-call(bf16[512,1024]{1,0:T(8,128)(2,1)} %context.1, ...), custom_call_target="tpu_custom_call" | custom-call | tf_op jit(solution)/shard_map/block/pallas_call | solution.py:1338
  128.0 4.2 %hand_on.1 = (bf16[512,1024]{1,0:T(8,128)(2,1)}, bf16[512,1024]{1,0:T(8,128)(2,1)}, bf16[512,1024]{1,0:T(8,128)(2,1)}, f32[512,384]{1,0:T(8,128)}, f32[96,512]{1...) custom-call(bf16[512,1024]{1,0:T(8,128)(2,1)} %get-tuple-element.27.refs_0_, ...), custom_call_target="tpu_custom_call" | custom-call | tf_op jit(solution)/shard_map/hand_on/pallas_call | solution.py:1440
